TPU v7x, 512 devices: a whole 4x4x16 slice. The times are simulated.
512 devices in a mesh: frames: 32 (over y, x, core), atoms: 16 (over z).
Axes of the slice: x: 4, y: 4, z: 16, core: 2. Of those that a mesh axis runs over, the one named last changes fastest.
Arguments:
- frames: float32 [2048, 3, 6144], P('frames', None, 'atoms'), may hold values from -45 to 45, as said below
- reference_structure: float32 [3, 6144], P(None, 'atoms'), may hold values from -15 to 15
Outputs:
- covariance: float32 [3, 6144, 3, 6144], P(None, 'frames', None, 'atoms')
- mean_structure: float32 [3, 6144], P(None, 'atoms')
Inputs may be any that keep to these rules, and one draw needn't show every extreme that they name: `frames`: every frame, once centered, has a cross-covariance with the centered reference_structure of positive determinant whose singular values lie within a factor of 20 of one another.
All inputs are finite; a program needn't handle non-finite values.
Results may differ from a plain program's by a relative error of at most 0.0003.
Values may be sent and summed in bfloat16 or wider, within the bound.
A program may use at most 64 MiB of HBM per device.

v0:
```python
import jax
import jax.numpy as jnp
from jax import lax
from jax.sharding import Mesh
from jax.sharding import PartitionSpec as P

ATOMS = 6144
ITERS = 2
POLAR = 8
FRAMES = ("frames_0", "frames_1", "frames_2")


def copy_for_each(array, axis):
    copies = jnp.broadcast_to(array, (lax.axis_size(axis), *array.shape))
    return lax.all_to_all(copies, axis, split_axis=0, concat_axis=0, tiled=True)


def over_copies(array, axis):
    everything = copy_for_each(array, axis)
    return jnp.sum(everything, axis=0)


def in_one(arrays, axis):
    vector, at, finished = (jnp.concatenate([a.reshape(-1) for a in arrays]), 0, [])
    total = over_copies(vector, axis)
    for a in arrays:
        finished.append(total[at : at + a.size].reshape(a.shape))
        at += a.size
    return tuple(finished)


def in_blocks(array, dim, devices):
    lengths = array.shape
    blocks = array.reshape(*lengths[:dim], devices, lengths[dim] // devices, *lengths[dim + 1 :])
    return jnp.moveaxis(blocks, dim, 0)


def laid_out(blocks, dim):
    blocks = jnp.moveaxis(blocks, 0, dim)
    lengths = blocks.shape
    return blocks.reshape(*lengths[:dim], lengths[dim] * lengths[dim + 1], *lengths[dim + 2 :])


def exchange_in_order(blocks, axes, turns):
    lengths = [lax.axis_size(a) for a in axes]
    blocks = blocks.reshape(*lengths, *blocks.shape[1:])
    for k in turns:
        blocks = lax.all_to_all(blocks, axes[k], split_axis=k, concat_axis=k, tiled=True)
    return blocks.reshape(-1, *blocks.shape[len(axes) :])


def core_and_chips(array, groups, turns, split_dim, concat_dim):
    devices = lax.axis_size(groups[0]) * lax.axis_size(groups[1])
    blocks = in_blocks(array, split_dim, devices)
    return laid_out(exchange_in_order(blocks, groups, turns), concat_dim)


def polar_factor(cross):
    factor = jnp.sqrt(3.0 / jnp.sum(cross * cross, axis=(0, 1)))
    matrix = cross * factor[None, None, :]
    for turn in range(POLAR):
        entries = [[matrix[i, j] for j in range(3)] for i in range(3)]
        cofactor = [
            [
                entries[(i + 1) % 3][(j + 1) % 3] * entries[(i + 2) % 3][(j + 2) % 3]
                - entries[(i + 1) % 3][(j + 2) % 3] * entries[(i + 2) % 3][(j + 1) % 3]
                for j in range(3)
            ]
            for i in range(3)
        ]
        determinant = (
            entries[0][0] * cofactor[0][0]
            + entries[0][1] * cofactor[0][1]
            + entries[0][2] * cofactor[0][2]
        )
        inverse = jnp.stack([jnp.stack(cofactor[i]) for i in range(3)]) / determinant[None, None, :]
        matrix = 0.5 * (matrix + inverse)
    return matrix


def contract_frames(left_rows, right_rows):
    return lax.dot_general(
        left_rows, right_rows, (((0,), (0,)), ((), ())), preferred_element_type=jnp.float32
    )


def body(frames, reference_structure):
    highest = lax.Precision.HIGHEST
    mean_now = reference_structure
    count_all = frames.shape[0] * lax.axis_size(FRAMES)
    for iteration in range(ITERS):
        sum_coords, sum_cross, sum_mean = in_one(
            (
                jnp.sum(frames, axis=2),
                jnp.einsum("fca,da->cdf", frames, mean_now, precision=highest),
                jnp.sum(mean_now, axis=1),
            ),
            "atoms",
        )
        centroid = sum_coords / ATOMS
        cross = sum_cross - centroid.T[:, None, :] * sum_mean[None, :, None]
        shifted = frames - centroid[:, :, None]
        rotation = polar_factor(cross)
        aligned = jnp.einsum("cdf,fca->fda", rotation, shifted, precision=highest)
        mean_now = over_copies(jnp.sum(aligned, axis=0), FRAMES) / count_all
    deviation = (aligned - mean_now[None]).astype(jnp.bfloat16)
    column_atoms = frames.shape[2]
    row_count = column_atoms * lax.axis_size("atoms") // lax.axis_size(FRAMES)
    own_rows = lax.all_gather(deviation, "atoms", axis=2, tiled=True)
    row_panel = core_and_chips(own_rows, (("frames_0", "frames_1"), "frames_2"), (1, 0), 2, 0)
    row_flat = row_panel.reshape(row_panel.shape[0], 3 * row_count)
    piece = lax.all_gather(deviation, FRAMES, axis=0, tiled=True)
    product = contract_frames(row_flat, piece.reshape(piece.shape[0], 3 * column_atoms))
    covariance = (product / count_all).reshape(3, row_count, 3, column_atoms)
    return (covariance, mean_now)


def solution(mesh):
    finer = Mesh(
        mesh.devices.reshape(4, 4, 2, mesh.shape["atoms"]),
        ("frames_0", "frames_1", "frames_2", "atoms"),
    )
    return jax.shard_map(
        body,
        mesh=finer,
        in_specs=(P(FRAMES, None, "atoms"), P(None, "atoms")),
        out_specs=(P(None, FRAMES, None, "atoms"), P(None, "atoms")),
        check_vma=False,
    )
```

profile of v0, /device:TPU:2, one launch (start us, length us, event | category | flops | bytes accessed | tf_op | source)
XLA Modules:
  0.0 281.3 jit_solution(8115866642797572257)
XLA Ops:
  7.2 0.8 reduce_sum.99
  8.1 1.1 reduce_sum.98
  9.1 1.4 convolution_bitcast_fusion.2
  10.6 0.1 reshape.5854
  10.7 0.1 copy.45
  10.8 0.1 reshape.5853
  11.0 0.1 fusion.26
  11.1 27.7 %all_to_all.32 = f32[16,1,771]{2,1,0:T(1,128)S(1)} all-to-all(f32[16,1,771]{2,1,0:T(1,128)S(1)} %broadcast_in_dim.8), channel_id=1, replica_groups=mesh['frames_0'=4,'frames_1'=4,'frames_2'=2,'atoms'=16] {'atoms'}, dimensions={0} | all-to-all | bytes 98688 | tf_op jit(solution)/shard_map/all_to_all | solution.py:15
  38.8 0.1 slice.472
  38.9 0.1 reshape.5855
  39.0 0.1 div.197
  39.1 0.1 copy.48
  39.2 0.1 copy.47
  39.3 0.1 multiply_reduce_fusion.1
  39.4 0.1 fusion.23
  39.5 0.1 fusion.7
  39.7 0.1 fusion.8
  39.9 0.1 fusion.9
  40.0 0.1 fusion.10
  40.2 0.1 fusion.11
  40.4 0.1 fusion.12
  40.5 0.1 fusion.13
  40.7 1.3 convolution_bitcast_fusion.1
  42.1 14.4 %all_to_all.33 = f32[32,3,384]{2,1,0:T(4,128)S(1)} all-to-all(f32[32,3,384]{2,1,0:T(4,128)S(1)} %broadcast_in_dim.9), channel_id=1, replica_groups=mesh['frames_0'=4,'frames_1'=4,'frames_2'=2,'atoms'=16] {'frames_0','fra..., dimensions={0} | all-to-all | bytes 294912 | tf_op jit(solution)/shard_map/all_to_all | solution.py:15
  56.6 0.1 multiply_reduce_fusion.2
  56.7 1.4 convolution_bitcast_fusion
  58.1 0.1 reshape.5856
  58.2 0.1 fusion.25
  58.4 15.9 %all_to_all.34 = f32[16,1,771]{2,1,0:T(1,128)S(1)} all-to-all(f32[16,1,771]{2,1,0:T(1,128)S(1)} %broadcast_in_dim.10), channel_id=1, replica_groups=mesh['frames_0'=4,'frames_1'=4,'frames_2'=2,'atoms'=16] {'atoms'}, dimensions={0} | all-to-all | bytes 98688 | tf_op jit(solution)/shard_map/all_to_all | solution.py:15
  74.3 0.1 slice.547
  74.4 0.1 reshape.5857
  74.5 0.1 div.225
  74.6 0.1 copy.52
  74.7 0.1 copy.51
  74.8 0.1 multiply_reduce_fusion
  74.9 0.1 fusion.24
  75.1 0.1 fusion.14
  75.2 0.1 fusion.15
  75.4 0.1 fusion.16
  75.5 0.1 fusion.17
  75.7 0.1 fusion.18
  75.9 0.1 fusion.19
  76.0 0.1 fusion.20
  76.2 0.1 fusion.21
  76.4 0.1 copy.53
  76.5 0.1 broadcast_subtract_fusion
  76.6 1.1 fusion.33
  77.7 11.5 %all_to_all.35 = f32[32,3,384]{2,1,0:T(4,128)S(1)} all-to-all(f32[32,3,384]{2,1,0:T(4,128)S(1)} %broadcast_in_dim.11), channel_id=1, replica_groups=mesh['frames_0'=4,'frames_1'=4,'frames_2'=2,'atoms'=16] {'frames_0','fra..., dimensions={0} | all-to-all | bytes 294912 | tf_op jit(solution)/shard_map/all_to_all | solution.py:15
  89.3 0.7 subtract_convert_fusion
  90.1 1.6 copy.60
  91.7 75.2 %all-gather.3.cloned.1.call-done = bf16[64,3,6144]{2,1,0:T(4,128)(2,1)} async-done(((bf16[64,3,384]{2,1,0:T(4,128)(2,1)}), bf16[64,3,6144]{2,1,0:T(4,128)(2,1)}) %all-gather.3.cloned.1.call-update) | async-done | bytes 2359312 | tf_op jit(solution)/shard_map/all_gather | solution.py:109
  166.9 3.6 %copy.56 = bf16[64,3,6144]{2,0,1:T(8,128)(2,1)S(1)} copy(bf16[64,3,6144]{2,1,0:T(4,128)(2,1)} %all-gather.3.cloned.1.call-done) | data formatting | bytes 4718592 | tf_op jit(solution)/shard_map/all_gather | solution.py:109
  170.5 4.6 %reshape.5858 = bf16[64,3,32,192]{3,2,0,1:T(8,128)(2,1)} reshape(bf16[64,3,6144]{2,0,1:T(8,128)(2,1)S(1)} %copy.56) | data formatting | bytes 4718592 | tf_op jit(solution)/shard_map/reshape | solution.py:34
  175.1 4.3 %reshape.5859 = bf16[16,2,64,3,192]{4,1,0,2,3:T(2,128)(2,1)S(1)} reshape(bf16[32,64,3,192]{3,0,1,2:T(8,128)(2,1)} %bitcast.395) | data formatting | bytes 4718592 | tf_op jit(solution)/shard_map/reshape | solution.py:46
  179.4 1.8 copy.57
  181.2 6.3 %all_to_all.36 = bf16[16,2,64,3,192]{4,2,3,0,1:T(8,128)(2,1)S(1)} all-to-all(bf16[16,2,64,3,192]{4,2,3,0,1:T(8,128)(2,1)S(1)} %copy.57), channel_id=1, replica_groups=mesh['frames_0'=4,'frames_1'=4,'frames_2'=2,'atoms'=16] {'frames_2'}, dimensions={1} | all-to-all | bytes 4718592 | tf_op jit(solution)/shard_map/all_to_all | solution.py:48
  187.4 0.4 copy.58
  187.8 53.9 %all_to_all.37 = bf16[16,2,64,3,192]{4,2,3,1,0:T(8,128)(2,1)S(1)} all-to-all(bf16[16,2,64,3,192]{4,2,3,1,0:T(8,128)(2,1)S(1)} %copy.58), channel_id=1, replica_groups=mesh['frames_0'=4,'frames_1'=4,'frames_2'=2,'atoms'=16] {'frames_0','fra..., dimensions={0} | all-to-all | bytes 4718592 | tf_op jit(solution)/shard_map/all_to_all | solution.py:48
  241.7 5.0 %copy.59 = bf16[16,2,64,3,192]{4,3,2,1,0:T(4,128)(2,1)} copy(bf16[16,2,64,3,192]{4,2,3,1,0:T(8,128)(2,1)S(1)} %all_to_all.37) | data formatting | bytes 4718592 | tf_op jit(solution)/shard_map/all_to_all | solution.py:48
  246.8 8.0 %reshape_reshape_reshape.3 = bf16[2048,576]{1,0:T(8,128)(2,1)S(1)} reshape(bf16[16,2,64,3,192]{4,3,2,1,0:T(4,128)(2,1)} %copy.59) | data formatting | bytes 4718592 | tf_op jit(solution)/shard_map/reshape;reshape;reshape | solution.py:111
  254.8 6.7 %copy.61 = bf16[2048,3,384]{0,2,1:T(8,128)(2,1)} copy(bf16[2048,3,384]{2,0,1:T(8,128)(2,1)} %all-gather.5.cloned.1.call-done) | data formatting | bytes 9437184 | tf_op jit(solution)/shard_map/all_gather | solution.py:112
  261.6 7.4 %convolution_multiply_fusion = f32[576,1152]{1,0:T(8,128)} fusion(bf16[2048,576]{1,0:T(8,128)(2,1)S(1)} %reshape_reshape_reshape.3, bf16[2048,1152]{0,1:T(8,128)(2,1)} %bitcast.396), kind=kOutput, calls=%fused_computation | convolution fusion | flops 2718572544 | bytes 9732096 | tf_op jit(solution)/shard_map/dot_general | solution.py:82
  269.0 3.7 %reshape.5861 = f32[3,192,3,384]{3,2,1,0:T(4,128)S(1)} reshape(f32[576,1152]{1,0:T(8,128)} %convolution_multiply_fusion) | data formatting | bytes 5308416 | tf_op jit(solution)/shard_map/reshape | solution.py:114
  272.7 1.7 copy.62
  (103 shorter events, 1.4 us)
Async XLA Ops:
  7.2 69.3 %copy-start = (f32[64,3,384]{2,0,1:T(8,128)S(1)}, f32[64,3,384]{2,0,1:T(8,128)}, u32[]{:S(2)}) copy-start(f32[64,3,384]{2,0,1:T(8,128)} %param.2) | copy-start | bytes 884740
  7.2 159.8 %all-gather.3.cloned.1.call-start = ((), (), s32[]{:S(2)}) async-start(), calls=%async_computation.6 | async-start | bytes 3342336 | tf_op jit(solution)/shard_map/all_gather | solution.py:109
  89.3 81.3 %copy-start.1 = (f32[3,384]{1,0:T(4,128)}, f32[3,384]{1,0:T(4,128)S(1)}, u32[]{:S(2)}) copy-start(f32[3,384]{1,0:T(4,128)S(1)} %broadcast_multiply_fusion) | copy-start | bytes 13828
  90.1 164.8 %all-gather.5.cloned.1.call-start = ((), (), s32[]{:S(2)}) async-start(), calls=%async_computation.7 | async-start | bytes 4866048 | tf_op jit(solution)/shard_map/all_gather | solution.py:112
Sparse Core Ops, SparseCore 0:
  90.2 76.7 all-gather.2
  170.1 73.4 all-gather.4
where the time goes:
time: 282 us; the launch traced here: 281 us
  blocking collectives  130 us (46%)
  waiting for transfers between devices  75.2 us (27%)
  local copies, waits for them, and re-layouts  43.1 us (15%)
  between operations  14.7 us (5%)
  matrix products  12.7 us (5%)
  other arithmetic  5.79 us (2%)
    all_gather x1, waiting for transfers between devices, body(): own_rows = lax.all_gather(deviation, 'atoms', axis=2, tiled=True)  75.2 us
    all_to_all x4, blocking collectives, copy_for_each(): return lax.all_to_all(copies, axis, split_axis=0, concat_axis=0, tiled=True)  69.5 us
    all_to_all x2, blocking collectives, exchange_in_order(): lax.all_to_all(blocks, axes[k], split_axis=k, concat_axis=k, tiled=True)  60.2 us
    another operation x1, local copies, waits for them, and re-layouts, body(): row_flat = row_panel.reshape(row_panel.shape[0], 3 * row_count)  8.03 us
    dot_general x1, matrix products, contract_frames(): lax.dot_general(left_rows, right_rows, (((0,), (0,)), ((), ())), preferre...  7.42 us
    all_gather x1, local copies, waits for them, and re-layouts, body(): piece = lax.all_gather(deviation, FRAMES, axis=0, tiled=True)  6.75 us
    reshape x2, local copies, waits for them, and re-layouts, exchange_in_order(): blocks = blocks.reshape(*lengths, *blocks.shape[1:])  6.04 us
  transfers between devices with their start and end apart: 2, of which 1 were waited for; matrix products, arithmetic and copies ran while one was open for 10% of the time, Pallas kernels for 0%

commit v1 on v0

--- a/solution.py
+++ b/solution.py
@@ -106,7 +106,9 @@
     deviation = (aligned - mean_now[None]).astype(jnp.bfloat16)
     column_atoms = frames.shape[2]
     row_count = column_atoms * lax.axis_size("atoms") // lax.axis_size(FRAMES)
-    own_rows = lax.all_gather(deviation, "atoms", axis=2, tiled=True)
+    own_rows = jnp.concatenate(
+        lax.all_to_all(jnp.stack([deviation] * lax.axis_size("atoms")), "atoms", 0, 0), axis=2
+    )
     row_panel = core_and_chips(own_rows, (("frames_0", "frames_1"), "frames_2"), (1, 0), 2, 0)
     row_flat = row_panel.reshape(row_panel.shape[0], 3 * row_count)
     piece = lax.all_gather(deviation, FRAMES, axis=0, tiled=True)

time: 282 us -> 311 us (1.10)
  the two profiles are of different devices: /device:TPU:2 before, /device:TPU:1 now
where the time goes in v1:
time: 311 us; the launch traced here: 310 us
  waiting for transfers between devices  144 us (46%)
  blocking collectives  78.6 us (25%)
  local copies, waits for them, and re-layouts  45.1 us (15%)
  between operations  14.7 us (5%)
  matrix products  12.7 us (4%)
  starting transfers between devices  9.78 us (3%)
  other arithmetic  5.13 us (2%)
    all_to_all x1, waiting for transfers between devices, body(): lax.all_to_all(jnp.stack([deviation] * lax.axis_size('atoms')), 'atoms',...  103 us
    all_to_all x4, blocking collectives, copy_for_each(): return lax.all_to_all(copies, axis, split_axis=0, concat_axis=0, tiled=True)  71.7 us
    all_to_all x1, waiting for transfers between devices, exchange_in_order(): lax.all_to_all(blocks, axes[k], split_axis=k, concat_axis=k, tiled=True)  40.8 us
    another operation x1, local copies, waits for them, and re-layouts, body(): row_flat = row_panel.reshape(row_panel.shape[0], 3 * row_count)  8.03 us
    dot_general x1, matrix products, contract_frames(): lax.dot_general(left_rows, right_rows, (((0,), (0,)), ((), ())), preferre...  7.42 us
    all_to_all x2, local copies, waits for them, and re-layouts, exchange_in_order(): lax.all_to_all(blocks, axes[k], split_axis=k, concat_axis=k, tiled=True)  7.03 us
    all_to_all x1, blocking collectives, exchange_in_order(): lax.all_to_all(blocks, axes[k], split_axis=k, concat_axis=k, tiled=True)  6.86 us
    all_gather x1, local copies, waits for them, and re-layouts, body(): piece = lax.all_gather(deviation, FRAMES, axis=0, tiled=True)  6.73 us
  transfers between devices with their start and end apart: 3, of which 2 were waited for; matrix products, arithmetic and copies ran while one was open for 7% of the time, Pallas kernels for 0%

profile of v1, /device:TPU:1, one launch (start us, length us, event | category | flops | bytes accessed | tf_op | source)
XLA Modules:
  0.0 310.3 jit_solution(6222511275006475489)
XLA Ops:
  7.2 0.9 reduce_sum.99
  8.0 1.1 reduce_sum.98
  9.1 1.4 convolution_bitcast_fusion.2
  10.5 0.1 reshape.5856
  10.7 0.1 copy.60
  10.8 0.1 reshape.5855
  10.9 0.1 fusion.26
  11.0 27.2 %all_to_all.37 = f32[16,1,771]{2,1,0:T(1,128)S(1)} all-to-all(f32[16,1,771]{2,1,0:T(1,128)S(1)} %broadcast_in_dim.8), channel_id=1, replica_groups=mesh['frames_0'=4,'frames_1'=4,'frames_2'=2,'atoms'=16] {'atoms'}, dimensions={0} | all-to-all | bytes 98688 | tf_op jit(solution)/shard_map/all_to_all | solution.py:15
  38.3 0.1 slice.472
  38.4 0.1 reshape.5857
  38.4 0.1 div.197
  38.6 0.1 copy.63
  38.7 0.1 multiply_reduce_fusion.1
  38.8 0.1 fusion.23
  39.0 0.1 fusion.7
  39.2 0.1 fusion.8
  39.3 0.1 fusion.9
  39.5 0.1 fusion.10
  39.6 0.1 fusion.11
  39.8 0.1 fusion.12
  40.0 0.1 fusion.13
  40.2 1.3 convolution_bitcast_fusion.1
  41.5 17.2 %all_to_all.38 = f32[32,3,384]{2,1,0:T(4,128)S(1)} all-to-all(f32[32,3,384]{2,1,0:T(4,128)S(1)} %broadcast_in_dim.9), channel_id=1, replica_groups=mesh['frames_0'=4,'frames_1'=4,'frames_2'=2,'atoms'=16] {'frames_0','fra..., dimensions={0} | all-to-all | bytes 294912 | tf_op jit(solution)/shard_map/all_to_all | solution.py:15
  58.8 0.1 multiply_reduce_fusion.2
  58.9 1.4 convolution_bitcast_fusion
  60.3 0.1 reshape.5858
  60.4 0.1 fusion.25
  60.6 14.2 %all_to_all.39 = f32[16,1,771]{2,1,0:T(1,128)S(1)} all-to-all(f32[16,1,771]{2,1,0:T(1,128)S(1)} %broadcast_in_dim.10), channel_id=1, replica_groups=mesh['frames_0'=4,'frames_1'=4,'frames_2'=2,'atoms'=16] {'atoms'}, dimensions={0} | all-to-all | bytes 98688 | tf_op jit(solution)/shard_map/all_to_all | solution.py:15
  74.8 0.1 slice.547
  74.9 0.1 reshape.5859
  75.0 0.1 div.225
  75.1 0.1 copy.67
  75.3 0.1 multiply_reduce_fusion
  75.4 0.1 fusion.24
  75.6 0.1 fusion.14
  75.7 0.1 fusion.15
  75.9 0.1 fusion.16
  76.0 0.1 fusion.17
  76.2 0.1 fusion.18
  76.4 0.1 fusion.19
  76.5 0.1 fusion.20
  76.7 0.1 fusion.21
  76.8 0.1 copy.68
  77.0 0.1 broadcast_subtract_fusion
  77.1 1.1 fusion.33
  78.2 13.2 %all_to_all.40 = f32[32,3,384]{2,1,0:T(4,128)S(1)} all-to-all(f32[32,3,384]{2,1,0:T(4,128)S(1)} %broadcast_in_dim.11), channel_id=1, replica_groups=mesh['frames_0'=4,'frames_1'=4,'frames_2'=2,'atoms'=16] {'frames_0','fra..., dimensions={0} | all-to-all | bytes 294912 | tf_op jit(solution)/shard_map/all_to_all | solution.py:15
  91.6 1.8 stack.611
  93.4 3.7 %all-to-all-start.4 = ((bf16[16,64,3,384]{3,1,2,0:T(8,128)(2,1)}), bf16[16,64,3,384]{3,1,2,0:T(8,128)(2,1)S(1)}, u32[]{:S(2)}, u32[]{:S(2)}) async-start(bf16[16,64,3,384]{3,1,2,0:T(8,128)(2,1)} %stack.611), calls=%async_computation.4 | async-start | bytes 4718592 | tf_op jit(solution)/shard_map/all_to_all | solution.py:110
  97.2 0.7 all-gather.2.cloned.1.call-update
  97.9 102.7 %all-to-all-done.4 = bf16[16,64,3,384]{3,1,2,0:T(8,128)(2,1)S(1)} async-done(((bf16[16,64,3,384]{3,1,2,0:T(8,128)(2,1)}), bf16[16,64,3,384]{3,1,2,0:T(8,128)(2,1)S(1)}, u32[]{:S(2)}, u32[]{:S(2)}) %all-to-all-start.4) | async-done | bytes 2359328 | tf_op jit(solution)/shard_map/all_to_all | solution.py:110
  200.6 2.8 copy.72
  203.4 5.6 %reshape_reshape.3 = bf16[64,3,32,192]{3,2,1,0:T(8,128)(2,1)} reshape(bf16[64,3,16,384]{3,2,1,0:T(8,128)(2,1)} %copy.72) | data formatting | bytes 4718592 | tf_op jit(solution)/shard_map/reshape;reshape | solution.py:34
  209.0 4.3 %reshape.5861 = bf16[16,2,64,3,192]{4,1,0,3,2:T(2,128)(2,1)S(1)} reshape(bf16[32,64,3,192]{3,0,2,1:T(8,128)(2,1)} %bitcast.396) | data formatting | bytes 4718592 | tf_op jit(solution)/shard_map/reshape | solution.py:46
  213.3 1.8 copy.73
  215.1 6.9 %all_to_all.41 = bf16[16,2,64,3,192]{4,2,3,0,1:T(8,128)(2,1)S(1)} all-to-all(bf16[16,2,64,3,192]{4,2,3,0,1:T(8,128)(2,1)S(1)} %copy.73), channel_id=1, replica_groups=mesh['frames_0'=4,'frames_1'=4,'frames_2'=2,'atoms'=16] {'frames_2'}, dimensions={1} | all-to-all | bytes 4718592 | tf_op jit(solution)/shard_map/all_to_all | solution.py:48
  221.9 2.1 copy.74
  224.0 6.0 %all-to-all-start.6 = ((bf16[16,2,64,3,192]{4,2,3,1,0:T(8,128)(2,1)}), bf16[16,2,64,3,192]{4,2,3,1,0:T(8,128)(2,1)S(1)}, u32[]{:S(2)}, u32[]{:S(2)}) async-start(bf16[16,2,64,3,192]{4,2,3,1,0:T(8,128)(2,1)} %copy.74), calls=%async_computation.6 | async-start | bytes 6291456 | tf_op jit(solution)/shard_map/all_to_all | solution.py:48
  230.0 6.7 %copy.77 = bf16[2048,3,384]{0,2,1:T(8,128)(2,1)} copy(bf16[2048,3,384]{2,0,1:T(8,128)(2,1)} %all-gather.2.cloned.1.call-done) | data formatting | bytes 9437184 | tf_op jit(solution)/shard_map/all_gather | solution.py:114
  236.8 40.8 %all-to-all-done.6 = bf16[16,2,64,3,192]{4,2,3,1,0:T(8,128)(2,1)S(1)} async-done(((bf16[16,2,64,3,192]{4,2,3,1,0:T(8,128)(2,1)}), bf16[16,2,64,3,192]{4,2,3,1,0:T(8,128)(2,1)S(1)}, u32[]{:S(2)}, u32[]{:S(2)}) %all-to-all-start.6) | async-done | bytes 2359328 | tf_op jit(solution)/shard_map/all_to_all | solution.py:48
  277.6 5.0 %copy.75 = bf16[16,2,64,3,192]{4,3,2,1,0:T(4,128)(2,1)} copy(bf16[16,2,64,3,192]{4,2,3,1,0:T(8,128)(2,1)S(1)} %all-to-all-done.6) | data formatting | bytes 4718592 | tf_op jit(solution)/shard_map/all_to_all | solution.py:48
  282.5 8.0 %reshape_reshape_reshape.3 = bf16[2048,576]{1,0:T(8,128)(2,1)S(1)} reshape(bf16[16,2,64,3,192]{4,3,2,1,0:T(4,128)(2,1)} %copy.75) | data formatting | bytes 4718592 | tf_op jit(solution)/shard_map/reshape;reshape;reshape | solution.py:113
  290.6 7.4 %convolution_multiply_fusion = f32[576,1152]{1,0:T(8,128)} fusion(bf16[2048,576]{1,0:T(8,128)(2,1)S(1)} %reshape_reshape_reshape.3, bf16[2048,1152]{0,1:T(8,128)(2,1)} %bitcast.398), kind=kOutput, calls=%fused_computation | convolution fusion | flops 2718572544 | bytes 9732096 | tf_op jit(solution)/shard_map/dot_general | solution.py:82
  298.0 3.7 %reshape.5863 = f32[3,192,3,384]{3,2,1,0:T(4,128)S(1)} reshape(f32[576,1152]{1,0:T(8,128)} %convolution_multiply_fusion) | data formatting | bytes 5308416 | tf_op jit(solution)/shard_map/reshape | solution.py:116
  301.8 1.7 copy.78
  (106 shorter events, 1.5 us)
Async XLA Ops:
  7.2 69.8 %copy-start = (f32[64,3,384]{2,0,1:T(8,128)S(1)}, f32[64,3,384]{2,0,1:T(8,128)}, u32[]{:S(2)}) copy-start(f32[64,3,384]{2,0,1:T(8,128)} %param.2) | copy-start | bytes 884740
  91.5 1.9 copy-start.2
  91.6 1.8 copy-start.1
  93.4 107.2 %all-to-all-start.4 = ((bf16[16,64,3,384]{3,1,2,0:T(8,128)(2,1)}), bf16[16,64,3,384]{3,1,2,0:T(8,128)(2,1)S(1)}, u32[]{:S(2)}, u32[]{:S(2)}) async-start(bf16[16,64,3,384]{3,1,2,0:T(8,128)(2,1)} %stack.611), calls=%async_computation.4 | async-start | bytes 4718592 | tf_op jit(solution)/shard_map/all_to_all | solution.py:110
  97.1 132.9 %all-gather.2.cloned.1.call-start = ((), (), s32[]{:S(2)}) async-start(), calls=%async_computation.7 | async-start | bytes 4866048 | tf_op jit(solution)/shard_map/all_gather | solution.py:114
  224.0 53.6 %all-to-all-start.6 = ((bf16[16,2,64,3,192]{4,2,3,1,0:T(8,128)(2,1)}), bf16[16,2,64,3,192]{4,2,3,1,0:T(8,128)(2,1)S(1)}, u32[]{:S(2)}, u32[]{:S(2)}) async-start(bf16[16,2,64,3,192]{4,2,3,1,0:T(8,128)(2,1)} %copy.74), calls=%async_computation.6 | async-start | bytes 6291456 | tf_op jit(solution)/shard_map/all_to_all | solution.py:48
Sparse Core Ops, SparseCore 0:
  101.1 59.8 all-gather.1
